TPU v7x, 128 devices: a whole 4x4x4 slice. The times are simulated.
128 devices in a mesh: dp: 4 (over z), seq: 32 (over x, y, core).
Axes of the slice: x: 4, y: 4, z: 4, core: 2. Of those that a mesh axis runs over, the one named last changes fastest.
Arguments:
- group_samples: bfloat16 [4, 32, 193, 2560], P('dp', 'seq'), may hold values from -6 to 6
- group_lengths: int32 [4, 32], P('dp', 'seq'), may hold values from 64 to 192, as said below
- group_offsets: int32 [4, 32], P('dp', 'seq'), may hold values from 0 to 4032, as said below
- conv_first: bfloat16 [80, 512], replicated, may hold values from -0.625 to 0.625
- conv_middle: bfloat16 [4, 1536, 512], replicated, may hold values from -0.15625 to 0.15625
- conv_last: bfloat16 [2, 1024, 512], replicated, may hold values from -0.1875 to 0.1875
- feat_gain: float32 [512], replicated, may hold values from 0.1 to 1.9
- proj_weight: bfloat16 [512, 1280], replicated, may hold values from -0.25 to 0.25
- proj_bias: float32 [1280], replicated, may hold values from -3 to 3
- attn_gain: float32 [1280], replicated, may hold values from 0.1 to 1.9
- attn_weight: bfloat16 [1280, 2560], P(None, ('dp', 'seq'))
Outputs:
- encoded: bfloat16 [4, 4096, 1280], P('dp', 'seq')
Inputs may be any that keep to these rules, and one draw needn't show every extreme that they name: `group_lengths`: each group has 64 to 192 frames and in every night some group has exactly 192. Groups 2 k and 2 k + 1 of a night together have 2 * 128 frames. The last group of every night has 64 frames. `group_offsets`: groups lie in frame order, end to end: group 2 k starts at frame 2 k * 128 and group 2 k + 1 starts where group 2 k ends.
All inputs are finite; a program needn't handle non-finite values.
Results may differ from a plain program's by a relative error of at most 0.035.
Values may be sent and summed in bfloat16 or wider, within the bound.
A program may use at most 192 MiB of HBM per device.

v0:
```python
import functools

import jax
import jax.numpy as jnp
from jax import lax
from jax.experimental import pallas as pl
from jax.experimental.pallas import tpu as pltpu
from jax.sharding import PartitionSpec as P

HEADS = 8
FR = 128
CH = 512
TAIL = 16
SWAP = 80
BF = jnp.bfloat16
F32 = jnp.float32


def dot(a, b):
    return jnp.dot(a, b, preferred_element_type=F32)


def row_norm(v, eps):
    center = jnp.mean(v, axis=-1, keepdims=True)
    d = v - center
    spread = jnp.mean(d * d, axis=-1, keepdims=True)
    return d * lax.rsqrt(spread + eps)


def settle(acc, rows, eps, out):
    for r in range(0, rows, 64):
        n = min(64, rows - r)
        v = acc[r : r + n, :]
        center = jnp.mean(v, axis=-1, keepdims=True)
        d = v - center
        spread = jnp.mean(d * d, axis=-1, keepdims=True)
        u = d * lax.rsqrt(2.0 * spread + 2.0 * eps)
        out(r, n, (u + u * lax.erf(u)).astype(BF))


def conv_kernel(
    meta, own, arr, first, middle_hbm, last_hbm, gain, proj_hbm, bias, attn_gain,
    hidden_ref, normed_ref,
    x, a1, a2, a3, a4, a5, a6, t1, t2, t3, t4, acc0, acc1, middle, last, proj, sems,
):
    copies = [
        pltpu.make_async_copy(middle_hbm.at[l], middle.at[l], sems.at[l]) for l in range(4)
    ]
    copies.append(pltpu.make_async_copy(last_hbm, last, sems.at[4]))
    copies.append(pltpu.make_async_copy(proj_hbm, proj, sems.at[5]))
    for copy in copies:
        copy.start()

    is_odd = meta[0]
    even_len = meta[1]
    n1 = jnp.where(is_odd == 1, jnp.maximum(even_len - FR, 0), jnp.minimum(even_len, FR))
    own_rows = own.shape[0]

    def source(r):
        even = jnp.where(r < even_len, r, own_rows + r - even_len)
        odd = jnp.where(
            r + FR < even_len, own_rows + r + FR - (own_rows - SWAP), r + FR - even_len
        )
        return jnp.where(is_odd == 1, odd, even)

    def frame_of(shape):
        r = lax.broadcasted_iota(jnp.int32, shape, 0)
        return r

    def picks(width, base, step):
        r = lax.broadcasted_iota(jnp.int32, (FR + TAIL, width), 0)
        col = lax.broadcasted_iota(jnp.int32, (FR + TAIL, width), 1) + base
        src = jnp.where(
            r < FR, source(r) + step, source(jnp.where(r == FR, n1 - 1, FR - 1)) + 1
        )
        return (src == col).astype(F32).astype(BF)

    pick_own, pick_arr = picks(own_rows, 0, 0), picks(SWAP, own_rows, 0)
    for c in range(0, 2560, 512):
        x[:, c : c + 512] = (
            dot(pick_own, own[:, c : c + 512]) + dot(pick_arr, arr[:, c : c + 512])
        ).astype(BF)
    x[:, 2560:2688] = (
        dot(picks(own_rows, 0, 1), own[:, :128]) + dot(picks(SWAP, own_rows, 1), arr[:, :128])
    ).astype(BF)

    nr = lax.broadcasted_iota(jnp.int32, (FR, FR + TAIL), 0)
    nc = lax.broadcasted_iota(jnp.int32, (FR, FR + TAIL), 1)
    following = jnp.where(nr == n1 - 1, FR, jnp.where(nr == FR - 1, FR + 1, nr + 1))
    pick_next = (following == nc).astype(F32).astype(BF)

    def close(a, t):
        body = jnp.concatenate([a[0, :, :CH], t[0, :, :CH]], axis=0)
        a[a.shape[0] - 1, :, :CH] = dot(pick_next, body).astype(BF)

    def layer_one(u, acc, parity, half):
        offset = lax.rem(40 * u, 128)
        base = pl.multiple_of(40 * u - offset, 128)
        er = lax.broadcasted_iota(jnp.int32, (256, 80), 0)
        ec = lax.broadcasted_iota(jnp.int32, (256, 80), 1)
        weight = dot((er == ec + offset).astype(F32).astype(BF), first[...]).astype(BF)
        parts = [x[:FR, pl.ds(pl.multiple_of(base + 640 * b, 128), 256)] for b in range(4)]
        parts.append(x[FR:, pl.ds(base, 256)])
        acc[...] = dot(jnp.concatenate(parts, axis=0), weight)

        def out(r, n, val):
            if r < 4 * FR:
                a1[8 * (r // FR) + half, r % FR : r % FR + n, parity * CH : parity * CH + CH] = val
            else:
                t1[half, :, parity * CH : parity * CH + CH] = val

        settle(acc, 4 * FR + TAIL, 1e-5, out)

    def one_step(i, carry):
        layer_one(2 * i, acc0, 0, i)
        layer_one(2 * i + 1, acc1, 1, i)
        return carry

    lax.fori_loop(0, 8, one_step, 0)
    close(a1, t1)

    def three_taps(ain, start, count, rows, layer, acc):
        pairs = ain[pl.ds(start, count)].reshape(count * rows, 2 * CH)
        ahead = ain[pl.ds(start + 1, count), :, :CH].reshape(count * rows, CH)
        acc[: count * rows, :] = dot(
            jnp.concatenate([pairs, ahead], axis=1), middle[layer]
        )

    def main_chunk(ain, aout, layer, i, acc):
        three_taps(ain, 4 * i, 4, FR, layer, acc)

        def out(r, n, val):
            s = r // FR
            aout[2 * i + s // 2, r % FR : r % FR + n, (s % 2) * CH : (s % 2) * CH + CH] = val

        settle(acc, 4 * FR, 2e-5, out)

    def tail_chunk(tin, tout, layer, count, acc):
        three_taps(tin, 0, count, TAIL, layer, acc)

        def out(r, n, val):
            for k in range(n // TAIL):
                s = (r + k * TAIL) // TAIL
                tout[s // 2, :, (s % 2) * CH : (s % 2) * CH + CH] = val[k * TAIL : (k + 1) * TAIL]

        settle(acc, count * TAIL, 2e-5, out)

    def layer(ain, aout, tin, tout, index, chunks, tail_count):
        copies[index].wait()

        def step(i, carry):
            main_chunk(ain, aout, index, 2 * i, acc0)
            main_chunk(ain, aout, index, 2 * i + 1, acc1)
            return carry

        if chunks > 1:
            lax.fori_loop(0, chunks // 2, step, 0)
        else:
            main_chunk(ain, aout, index, 0, acc0)
        if tail_count:
            tail_chunk(tin, tout, index, tail_count, acc1)
            close(aout, tout)

    layer(a1, a2, t1, t2, 0, 8, 7)
    layer(a2, a3, t2, t3, 1, 4, 3)
    layer(a3, a4, t3, t4, 2, 2, 1)
    layer(a4, a5, None, None, 3, 1, 0)

    copies[4].wait()
    acc0[: 2 * FR, :] = dot(a5[...].reshape(2 * FR, 2 * CH), last[0])

    def out6(r, n, val):
        a6[r % FR : r % FR + n, (r // FR) * CH : (r // FR) * CH + CH] = val

    settle(acc0, 2 * FR, 2e-5, out6)
    acc1[:FR, :] = dot(a6[...], last[1])
    feats = []
    settle(acc1, FR, 2e-5, lambda r, n, val: feats.append(val))
    frame_feat = jnp.concatenate(feats, axis=0).astype(F32)
    normed_feat = (row_norm(frame_feat, 2e-5) * gain[...]).astype(BF)
    copies[5].wait()
    hidden = (dot(normed_feat, proj[...]) + bias[...]).astype(BF)
    hidden_ref[...] = hidden
    normed_ref[...] = (row_norm(hidden.astype(F32), 1e-5) * attn_gain[...]).astype(BF)


def conv_call(meta, own, arr, first, middle, last, gain, proj, bias, attn_gain):
    vmem = pl.BlockSpec(memory_space=pltpu.VMEM)
    hbm = pl.BlockSpec(memory_space=pl.ANY)
    width = proj.shape[1]
    return pl.pallas_call(
        conv_kernel,
        out_shape=[jax.ShapeDtypeStruct((FR, width), BF)] * 2,
        in_specs=[
            pl.BlockSpec(memory_space=pltpu.SMEM), vmem, vmem, vmem, hbm, hbm, vmem, hbm, vmem, vmem,
        ],
        out_specs=[vmem] * 2,
        scratch_shapes=[
            pltpu.VMEM((FR + TAIL, 2688), BF),
            pltpu.VMEM((33, FR, 2 * CH), BF),
            pltpu.VMEM((17, FR, 2 * CH), BF),
            pltpu.VMEM((9, FR, 2 * CH), BF),
            pltpu.VMEM((5, FR, 2 * CH), BF),
            pltpu.VMEM((2, FR, 2 * CH), BF),
            pltpu.VMEM((FR, 2 * CH), BF),
            pltpu.VMEM((8, TAIL, 2 * CH), BF),
            pltpu.VMEM((4, TAIL, 2 * CH), BF),
            pltpu.VMEM((2, TAIL, 2 * CH), BF),
            pltpu.VMEM((1, TAIL, 2 * CH), BF),
            pltpu.VMEM((4 * FR + TAIL, CH), F32),
            pltpu.VMEM((4 * FR + TAIL, CH), F32),
            pltpu.VMEM(middle.shape, BF),
            pltpu.VMEM(last.shape, BF),
            pltpu.VMEM(proj.shape, BF),
            pltpu.SemaphoreType.DMA((6,)),
        ],
        compiler_params=pltpu.CompilerParams(vmem_limit_bytes=56 << 20),
        cost_estimate=pl.CostEstimate(
            flops=16 * 10**9, bytes_accessed=14 * 10**6, transcendentals=9 * 10**6
        ),
        name="conv_stack",
    )(
        meta, own, arr, first, middle, last, gain.reshape(1, -1), proj, bias.reshape(1, -1),
        attn_gain.reshape(1, -1),
    )


def partner(value, axis):
    pairs = [(source, source ^ 1) for source in range(lax.axis_size(axis))]
    return lax.ppermute(value, axis, pairs)


def body(
    group_samples, group_lengths, group_offsets, conv_first, conv_middle, conv_last,
    feat_gain, proj_weight, proj_bias, attn_gain, attn_weight,
):
    panels = lax.all_gather(attn_weight, ("dp", "seq"), axis=1, tiled=True)
    inner_width = panels.shape[1] // 4
    head_size = inner_width // HEADS
    is_odd = lax.axis_index("seq") % 2
    samples = group_samples[0, 0]
    rows = samples.shape[0]
    length = group_lengths[0, 0]
    even_len = jnp.where(is_odd == 1, 2 * FR - length, length)
    outgoing = jnp.where(is_odd == 1, samples[:SWAP], samples[rows - SWAP :])
    arrived = partner(outgoing, "seq")
    meta = jnp.stack([is_odd, even_len]).astype(jnp.int32)
    hidden_x, normed_x = conv_call(
        meta, samples, arrived, conv_first, conv_middle, conv_last, feat_gain, proj_weight,
        proj_bias, attn_gain,
    )
    projected = jnp.dot(
        normed_x, panels[:, : 3 * inner_width], preferred_element_type=F32
    ).astype(BF)
    queries = projected[:, :inner_width]
    keys_local = projected[:, inner_width : 2 * inner_width]
    values_local = projected[:, 2 * inner_width :]
    scale = 1.0 / jnp.sqrt(jnp.float32(head_size))
    queries3 = queries.reshape(FR, HEADS, head_size)
    key_piece = lax.all_gather(keys_local, "seq", axis=0, tiled=True).reshape(-1, HEADS, head_size)
    value_piece = lax.all_gather(values_local, "seq", axis=0, tiled=True).reshape(
        -1, HEADS, head_size
    )
    scores = (
        jnp.einsum("qhd,khd->hqk", queries3, key_piece, preferred_element_type=F32) * scale
    )
    peak = jnp.max(scores, axis=-1)
    expo = jnp.exp(scores - peak[:, :, None])
    total = jnp.sum(expo, axis=-1)
    accum = jnp.einsum("hqk,khd->hqd", expo.astype(BF), value_piece, preferred_element_type=F32)
    mixed = (
        jnp.transpose(accum / total[:, :, None], (1, 0, 2)).reshape(FR, inner_width).astype(BF)
    )
    out_proj = lax.dot_general(
        mixed, panels[:, 3 * inner_width :], (((1,), (1,)), ((), ())), preferred_element_type=F32
    )
    encoded = (hidden_x.astype(F32) + out_proj).astype(BF)
    return encoded.reshape(1, FR, -1)


def solution(mesh):
    in_specs = (
        P("dp", "seq", None, None), P("dp", "seq"), P("dp", "seq"),
        P(), P(), P(), P(), P(), P(), P(), P(None, ("dp", "seq")),
    )
    out_specs = P("dp", "seq", None)
    return jax.shard_map(body, mesh=mesh, in_specs=in_specs, out_specs=out_specs, check_vma=False)
```

profile of v0, /device:TPU:1, one launch (start us, length us, event | category | flops | bytes accessed | tf_op | source)
XLA Modules:
  0.0 221.0 jit_solution(10405318127149896151)
XLA Ops:
  6.5 0.7 all-gather.9.cloned.1.call-update
  7.3 1.3 select_bitcast_fusion
  8.6 1.5 collective-permute-start
  10.7 1.3 reshape.30.bias
  12.0 1.3 reshape.31.attn_gain
  13.3 0.6 pad_add_fusion.meta
  14.0 0.8 copy-done.1
  14.8 33.1 %conv_stack.1 = (bf16[128,1280]{1,0:T(8,128)(2,1)}, bf16[128,1280]{1,0:T(8,128)(2,1)}) custom-call(s32[2]{0:T(128)} %pad_add_fusion.meta, bf16[193,2560]{1,0:T(8,128)(2,1)} %bitcast.36, bf16[80,2560]{1,0:T(8,128)(2,1)} %copy-done.1, bf16[80,512]{1,0:T(8,128)(2,1)} %first.1, bf16[4,1536,512]{2,1,0:T(8,128)(2,1)} %middle_hbm.1, ...), custom_call_target="tpu_custom_call" | custom-call | flops 16000000000 | bytes 14000000 | tf_op jit(solution)/shard_map/conv_stack/pallas_call | solution.py:191
  47.9 36.0 %all-gather.9.cloned.1.call-done = bf16[128,20,1280]{2,1,0:T(8,128)(2,1)} async-done(((bf16[1,20,1280]{2,1,0:T(8,128)(2,1)}), bf16[128,20,1280]{2,1,0:T(8,128)(2,1)}) %all-gather.9.cloned.1.call-update) | async-done | bytes 6553616 | tf_op jit(solution)/shard_map/all_gather | solution.py:237
  83.9 10.6 %reshape.37 = bf16[2560,1280]{1,0:T(8,128)(2,1)} reshape(bf16[128,20,1280]{2,1,0:T(8,128)(2,1)} %all-gather.9.cloned.1.call-done) | data formatting | bytes 13107200
  94.5 4.1 %fusion.8 = bf16[128,1920]{1,0:T(8,128)(2,1)S(1)} fusion(bf16[128,1280]{1,0:T(8,128)(2,1)S(1)} %copy-done.2, bf16[1280,2560]{0,1:T(8,128)(2,1)} %bitcast.32), kind=kOutput, calls=%fused_computation.9 | convolution fusion | flops 629391360 | bytes 5734400 | tf_op jit(solution)/shard_map/dot_general | solution.py:252
  98.6 0.8 fusion.24
  99.4 0.2 all-gather.7.cloned.1.call-start
  99.6 0.5 all-gather.7.cloned.1.call-update
  100.1 0.2 copy.17
  100.3 44.1 %all-gather.5.cloned.1.call-done = bf16[4096,640]{1,0:T(8,128)(2,1)} async-done(((bf16[128,640]{1,0:T(8,128)(2,1)}), bf16[4096,640]{1,0:T(8,128)(2,1)}) %all-gather.5.cloned.1.call-update) | async-done | bytes 5242896 | tf_op jit(solution)/shard_map/all_gather | solution.py:260
  144.4 7.9 %copy.18 = bf16[4096,640]{0,1:T(8,128)(2,1)} copy(bf16[4096,640]{1,0:T(8,128)(2,1)} %all-gather.5.cloned.1.call-done) | data formatting | bytes 10485760 | tf_op jit(solution)/shard_map/all_gather | solution.py:260
  152.3 10.6 %multiply_reduce_fusion = (f32[8,128]{1,0:T(8,128)S(1)}, f32[8,128,4096]{2,1,0:T(8,128)}) fusion(bf16[128,8,80]{0,2,1:T(8,128)(2,1)S(1)} %bitcast.35, bf16[4096,8,80]{0,2,1:T(8,128)(2,1)} %bitcast.31), kind=kOutput, calls=%fused_computation.1 | convolution fusion | flops 679476224 | bytes 22188032 | tf_op jit(solution)/shard_map/qhd,khd->hqk/dot_general | solution.py:265
  162.9 8.7 %fusion = f32[8,128]{1,0:T(8,128)S(1)} fusion(f32[8,128,4096]{2,1,0:T(8,128)} %get-tuple-element.13, f32[8,128]{1,0:T(8,128)S(1)} %get-tuple-element.12), kind=kLoop, calls=%fused_computation.2 | loop fusion | flops 12581888 | bytes 16785408 | tf_op jit(solution)/shard_map/reduce_sum | solution.py:269
  171.6 21.8 %all-gather.7.cloned.1.call-done = bf16[4096,640]{1,0:T(8,128)(2,1)} async-done(((bf16[128,640]{1,0:T(8,128)(2,1)}), bf16[4096,640]{1,0:T(8,128)(2,1)}) %all-gather.7.cloned.1.call-update) | async-done | bytes 5242896 | tf_op jit(solution)/shard_map/all_gather | solution.py:261
  193.4 7.9 %copy.19 = bf16[4096,640]{0,1:T(8,128)(2,1)} copy(bf16[4096,640]{1,0:T(8,128)(2,1)} %all-gather.7.cloned.1.call-done) | data formatting | bytes 10485760 | tf_op jit(solution)/shard_map/all_gather | solution.py:261
  201.3 10.5 %fusion.19 = bf16[128,8,80]{0,2,1:T(8,128)(2,1)S(1)} fusion(bf16[4096,8,80]{0,2,1:T(8,128)(2,1)} %bitcast.34, f32[8,128,4096]{2,1,0:T(8,128)} %get-tuple-element.13, f32[8,128]{1,0:T(8,128)S(1)} %get-tuple-element.12, f32[128,8]{0,1:T(8,128)S(1)} %bitcast.39), kind=kOutput, calls=%fused_computation.14 | convolution fusion | flops 683835392 | bytes 22192128 | tf_op jit(solution)/shard_map/hqk,khd->hqd/dot_general | solution.py:270
  211.8 1.9 fusion.11
  213.7 0.8 fusion.22
  (9 shorter events, 0.1 us)
Async XLA Ops:
  6.5 77.4 %all-gather.9.cloned.1.call-start = ((), (), s32[]{:S(2)}) async-start(), calls=%async_computation.2 | async-start | bytes 7925760 | tf_op jit(solution)/shard_map/all_gather | solution.py:237
  7.3 137.1 %all-gather.5.cloned.1.call-start = ((), (), s32[]{:S(2)}) async-start(), calls=%async_computation | async-start | bytes 5406720 | tf_op jit(solution)/shard_map/all_gather | solution.py:260
  8.6 5.4 %collective-permute-start = (bf16[80,2560]{1,0:T(8,128)(2,1)S(1)}, bf16[80,2560]{1,0:T(8,128)(2,1)S(1)}, u32[]{:S(2)}, u32[]{:S(2)}) collective-permute-start(bf16[80,2560]{1,0:T(8,128)(2,1)S(1)} %select_bitcast_fusion), channel_id=1, source_target_pairs={{0,1},{1,0},{2,3},{3,2},{4,5},{5,4},{6,7},{7,6},{8,9},{9,8},{10,11... | collective-permute-start | bytes 1228808 | tf_op jit(solution)/shard_map/ppermute | solution.py:230
  14.0 0.8 copy-start.1
  47.9 46.6 %copy-start.2 = (bf16[128,1280]{1,0:T(8,128)(2,1)S(1)}, bf16[128,1280]{1,0:T(8,128)(2,1)}, u32[]{:S(2)}) copy-start(bf16[128,1280]{1,0:T(8,128)(2,1)} %get-tuple-element.8) | copy-start | bytes 983044
  99.4 94.0 %all-gather.7.cloned.1.call-start = ((), (), s32[]{:S(2)}) async-start(), calls=%async_computation.1 | async-start | bytes 5406720 | tf_op jit(solution)/shard_map/all_gather | solution.py:261
  201.3 12.4 %copy-start = (bf16[128,1280]{1,0:T(8,128)(2,1)S(1)}, bf16[128,1280]{1,0:T(8,128)(2,1)}, u32[]{:S(2)}) copy-start(bf16[128,1280]{1,0:T(8,128)(2,1)} %get-tuple-element.7) | copy-start | bytes 983044
Sparse Core Ops, SparseCore 0:
  10.5 73.3 all-gather.8
  99.5 44.7 all-gather.4
  146.6 46.6 all-gather.6
where the time goes:
time: 222 us; the launch traced here: 221 us
  waiting for transfers between devices  103 us (46%)
  Pallas kernels  33.1 us (15%)
  local copies, waits for them, and re-layouts  30.8 us (14%)
  matrix products  27.1 us (12%)
  between operations  13.8 us (6%)
  other arithmetic  11.3 us (5%)
    all_gather x1, waiting for transfers between devices, body(): lax.all_gather(keys_local, 'seq', axis=0, tiled=True)  44.1 us
    all_gather x1, waiting for transfers between devices, body(): panels = lax.all_gather(attn_weight, ('dp', 'seq'), axis=1, tiled=True)  36 us
    pallas_call x1, Pallas kernels, conv_call(): pl.pallas_call(conv_kernel, out_shape=[jax.ShapeDtypeStruct((FR, width),...  33.1 us
    all_gather x1, waiting for transfers between devices, body(): lax.all_gather(values_local, 'seq', axis=0, tiled=True)  21.8 us
    unnamed x7, local copies, waits for them, and re-layouts  11.4 us
    dot_general x1, matrix products, body(): jnp.einsum('qhd,khd->hqk', queries3, key_piece, preferred_element_type=F32)  10.6 us
    dot_general x1, matrix products, body(): jnp.einsum('hqk,khd->hqd', expo.astype(BF), value_piece, preferred_elemen...  10.5 us
    reduce_sum x1, other arithmetic, body(): total = jnp.sum(expo, axis=-1)  8.67 us
  transfers between devices with their start and end apart: 4, of which 3 were waited for; matrix products, arithmetic and copies ran while one was open for 14% of the time, Pallas kernels for 15%

commit v1 on v0

--- a/solution.py
+++ b/solution.py
@@ -1,4 +1,4 @@
-import functools
+import math
 
 import jax
 import jax.numpy as jnp
@@ -7,13 +7,12 @@
 from jax.experimental.pallas import tpu as pltpu
 from jax.sharding import PartitionSpec as P
 
-HEADS = 8
 FR = 128
 CH = 512
 TAIL = 16
-SWAP = 80
 BF = jnp.bfloat16
 F32 = jnp.float32
+SCALE = math.log2(math.e) / math.sqrt(80)
 
 
 def dot(a, b):
@@ -38,11 +37,72 @@
         out(r, n, (u + u * lax.erf(u)).astype(BF))
 
 
-def conv_kernel(
-    meta, own, arr, first, middle_hbm, last_hbm, gain, proj_hbm, bias, attn_gain,
-    hidden_ref, normed_ref,
-    x, a1, a2, a3, a4, a5, a6, t1, t2, t3, t4, acc0, acc1, middle, last, proj, sems,
+MESH = pl.DeviceIdType.MESH
+NT = (((1,), (1,)), ((), ()))
+
+
+def onehot(mask):
+    return mask.astype(F32).astype(BF)
+
+
+def kernel(
+    length, samples_hbm, shard, first, middle_hbm, last_hbm, gain, proj_hbm, bias, attn_gain,
+    out_ref,
+    own, arr, x, a1, a2, a3, a4, a5, a6, t1, t2, t3, t4, acc0, acc1, middle, last, proj,
+    zbuf, wblk, wbuf, normed2, hidden_buf, ysend, qkv, kvbuf, qs, peak, total, accum,
+    mout, mbuf, part, psend, precv, sems, send_sems, recv_sems,
 ):
+    me = lax.axis_index("seq")
+    night = lax.axis_index("dp")
+    core = me % 2
+    chip = me // 2
+    cx, cy = chip // 4, chip % 4
+    ha = jnp.where(core == 0, cy, cx)
+    qb = jnp.where(core == 0, cx, cy)
+    half = cx // 2
+    mate = me + 1 - 2 * core
+
+    def place(a, b):
+        return jnp.where(core == 0, (b * 4 + a) * 2, (a * 4 + b) * 2 + 1)
+
+    def remote(src, dst, k, r, device):
+        return pltpu.make_async_remote_copy(
+            src_ref=src, dst_ref=dst, send_sem=send_sems.at[k], recv_sem=recv_sems.at[r],
+            device_id=device, device_id_type=MESH,
+        )
+
+    barrier = pltpu.get_barrier_semaphore()
+
+    def greet(device):
+        pl.semaphore_signal(barrier, inc=1, device_id=device, device_id_type=MESH)
+
+    greet({"seq": mate})
+    for d in range(1, 4):
+        greet({"dp": (night + d) % 4})
+        greet({"seq": place((ha + d) % 4, qb)})
+        greet({"seq": place(ha, (qb + d) % 4)})
+    for k in range(16):
+        source = 16 * core + k
+
+        @pl.when(source != me)
+        def _():
+            greet({"seq": source})
+
+    in_set = jnp.where(half == core, 1, 0)
+    pl.semaphore_wait(barrier, 26 - in_set)
+
+    swap = remote(samples_hbm, arr, 20, 20, {"seq": mate})
+    swap.start()
+    zcopies = [
+        remote(shard, zbuf.at[night], 16 + d, 16 + (4 - d) % 4, {"dp": (night + d) % 4})
+        for d in range(1, 4)
+    ]
+    for copy in zcopies:
+        copy.start()
+    own_copy = pltpu.make_async_copy(samples_hbm, own, sems.at[6])
+    own_copy.start()
+    zown = pltpu.make_async_copy(shard, zbuf.at[night], sems.at[7])
+    zown.start()
     copies = [
         pltpu.make_async_copy(middle_hbm.at[l], middle.at[l], sems.at[l]) for l in range(4)
     ]
@@ -51,21 +111,18 @@
     for copy in copies:
         copy.start()
 
-    is_odd = meta[0]
-    even_len = meta[1]
+    is_odd = core
+    group_len = length[0, 0]
+    even_len = jnp.where(is_odd == 1, 2 * FR - group_len, group_len)
     n1 = jnp.where(is_odd == 1, jnp.maximum(even_len - FR, 0), jnp.minimum(even_len, FR))
     own_rows = own.shape[0]
 
     def source(r):
         even = jnp.where(r < even_len, r, own_rows + r - even_len)
         odd = jnp.where(
-            r + FR < even_len, own_rows + r + FR - (own_rows - SWAP), r + FR - even_len
+            r + FR < even_len, own_rows + r + FR, r + FR - even_len
         )
         return jnp.where(is_odd == 1, odd, even)
-
-    def frame_of(shape):
-        r = lax.broadcasted_iota(jnp.int32, shape, 0)
-        return r
 
     def picks(width, base, step):
         r = lax.broadcasted_iota(jnp.int32, (FR + TAIL, width), 0)
@@ -73,15 +130,42 @@
         src = jnp.where(
             r < FR, source(r) + step, source(jnp.where(r == FR, n1 - 1, FR - 1)) + 1
         )
-        return (src == col).astype(F32).astype(BF)
-
-    pick_own, pick_arr = picks(own_rows, 0, 0), picks(SWAP, own_rows, 0)
+        return onehot(src == col)
+
+    own_copy.wait()
+    zown.wait()
+    for copy in zcopies:
+        copy.wait_recv()
+    cr = lax.broadcasted_iota(jnp.int32, (80, 128), 0)
+    cc = lax.broadcasted_iota(jnp.int32, (80, 128), 1)
+    wblk[...] = dot(
+        onehot(cc == 32 * (cr // 20) + cr % 20), zbuf[...].reshape(128, zbuf.shape[2])
+    ).astype(BF)
+    slot = me - 16 * half
+
+    def weight_copy(k):
+        target = ((chip + k) % 16) * 2 + half
+        return target, remote(wblk, wbuf.at[slot], k, slot, {"seq": target})
+
+    for k in range(16):
+        target, copy = weight_copy(k)
+
+        @pl.when(target != me)
+        def _():
+            copy.start()
+
+    @pl.when(half == core)
+    def _():
+        wbuf[slot] = wblk[...]
+
+    swap.wait_recv()
+    pick_own, pick_arr = picks(own_rows, 0, 0), picks(own_rows, own_rows, 0)
     for c in range(0, 2560, 512):
         x[:, c : c + 512] = (
             dot(pick_own, own[:, c : c + 512]) + dot(pick_arr, arr[:, c : c + 512])
         ).astype(BF)
     x[:, 2560:2688] = (
-        dot(picks(own_rows, 0, 1), own[:, :128]) + dot(picks(SWAP, own_rows, 1), arr[:, :128])
+        dot(picks(own_rows, 0, 1), own[:, :128]) + dot(picks(own_rows, own_rows, 1), arr[:, :128])
     ).astype(BF)
 
     nr = lax.broadcasted_iota(jnp.int32, (FR, FR + TAIL), 0)
@@ -180,23 +264,160 @@
     normed_feat = (row_norm(frame_feat, 2e-5) * gain[...]).astype(BF)
     copies[5].wait()
     hidden = (dot(normed_feat, proj[...]) + bias[...]).astype(BF)
-    hidden_ref[...] = hidden
-    normed_ref[...] = (row_norm(hidden.astype(F32), 1e-5) * attn_gain[...]).astype(BF)
-
-
-def conv_call(meta, own, arr, first, middle, last, gain, proj, bias, attn_gain):
+    hidden_buf[...] = hidden
+    normed2[pl.ds(pl.multiple_of(core * FR, FR), FR), :] = (
+        row_norm(hidden.astype(F32), 1e-5) * attn_gain[...]
+    ).astype(BF)
+    mine = normed2.at[pl.ds(pl.multiple_of(core * FR, FR), FR)]
+    exchange = remote(mine, mine, 21, 21, {"seq": mate})
+    exchange.start()
+    for k in range(16):
+
+        @pl.when(16 * core + k != me)
+        def _():
+            remote(wblk, wbuf.at[k], 0, k, {"seq": mate}).wait_recv()
+
+    exchange.wait_recv()
+
+    yr = lax.broadcasted_iota(jnp.int32, (320, 1), 0)
+    row_scale = jnp.where(yr % 80 < 20, SCALE, 1.0).astype(F32)
+    pr = lax.broadcasted_iota(jnp.int32, (240, 320), 0)
+    pc = lax.broadcasted_iota(jnp.int32, (240, 320), 1)
+    regroup = onehot(pc == 80 * ((pr % 80) // 20) + 20 * (pr // 80) + pr % 20)
+
+    def project(h, carry):
+        w = wbuf[pl.ds(4 * h, 4)].reshape(320, wbuf.shape[2])
+        y = lax.dot_general(w, normed2[...], NT, preferred_element_type=F32)
+        ysend[h] = dot(regroup, (y * row_scale).astype(BF)).astype(BF)
+        return carry
+
+    lax.fori_loop(0, 4, project, 0)
+
+    heads = []
+    for d in range(1, 4):
+        to = (ha + d) % 4
+        heads.append(
+            remote(ysend.at[to], qkv.at[ha], 24 + d, 24 + (4 - d) % 4, {"seq": place(to, qb)})
+        )
+        heads[-1].start()
+    keep = pltpu.make_async_copy(ysend.at[ha], qkv.at[ha], sems.at[8])
+    keep.start()
+
+    forwards = []
+
+    def forward(d):
+        src = qkv.at[(ha + d) % 4, pl.ds(80, 160)]
+        for e in range(1, 4):
+            copy = remote(
+                src, kvbuf.at[qb, (ha + d) % 4], 28 + 4 * d + e, 28 + 4 * d + (4 - e) % 4,
+                {"seq": place(ha, (qb + e) % 4)},
+            )
+            copy.start()
+            forwards.append(copy)
+
+    keep.wait()
+    forward(0)
+    for d in (3, 1, 2):
+        remote(ysend.at[0], qkv.at[(ha + d) % 4], 24, 24 + d, {"seq": mate}).wait_recv()
+        forward(d)
+
+    mout[...] = jnp.zeros_like(mout)
+    for i in range(4):
+        qs[i] = jnp.transpose(qkv[i, :80, :].astype(F32)).astype(BF)
+
+    def attend(keys, values, is_first):
+        def step(i, carry):
+            s = dot(qs[i], keys)
+            top = jnp.max(s, axis=-1, keepdims=True)
+            if not is_first:
+                top = jnp.maximum(top, peak[i])
+            p = jnp.exp2(s - top)
+            mass = jnp.sum(p, axis=-1, keepdims=True)
+            o = lax.dot_general(p.astype(BF), values, NT, preferred_element_type=F32)
+            if not is_first:
+                fade = jnp.exp2(peak[i] - top)
+                mass = mass + total[i] * fade
+                o = o + accum[i] * fade
+            peak[i] = top
+            total[i] = mass
+            accum[i] = o
+            return carry
+
+        lax.fori_loop(0, 4, step, 0)
+
+    attend(
+        jnp.concatenate([qkv[i, 80:160, :] for i in range(4)], axis=1),
+        jnp.concatenate([qkv[i, 160:240, :] for i in range(4)], axis=1),
+        True,
+    )
+    for e in (1, 3, 2):
+        b = (qb + e) % 4
+        for d in range(4):
+            remote(
+                qkv.at[0, pl.ds(80, 160)], kvbuf.at[b, (ha + d) % 4], 28, 28 + 4 * d + e,
+                {"seq": mate},
+            ).wait_recv()
+        attend(
+            jnp.concatenate([kvbuf[b, i, :80, :] for i in range(4)], axis=1),
+            jnp.concatenate([kvbuf[b, i, 80:, :] for i in range(4)], axis=1),
+            False,
+        )
+    for i in range(4):
+        mout[i, :, :80] = (accum[i] / total[i]).astype(BF)
+    returns = []
+    for d in range(1, 4):
+        to = (ha + d) % 4
+        returns.append(
+            remote(mout.at[to], mbuf.at[ha], 44 + d, 44 + (4 - d) % 4, {"seq": place(to, qb)})
+        )
+        returns[-1].start()
+    keep2 = pltpu.make_async_copy(mout.at[ha], mbuf.at[ha], sems.at[9])
+    keep2.start()
+    er = lax.broadcasted_iota(jnp.int32, (128, 320), 0)
+    ec = lax.broadcasted_iota(jnp.int32, (128, 320), 1)
+    spread = onehot((ec == 80 * (er // 20) + 60 + er % 20) & (er < 80))
+    keep2.wait()
+    for d in range(1, 4):
+        remote(mout.at[0], mbuf.at[(ha + d) % 4], 44, 44 + d, {"seq": mate}).wait_recv()
+    sums = None
+    for h in range(4):
+        wide = dot(mbuf[h], spread).astype(BF)
+        term = dot(wide, wbuf[4 * h : 4 * h + 4].reshape(320, wbuf.shape[2]))
+        sums = term if sums is None else sums + term
+    part[...] = sums.reshape(2, FR, sums.shape[1])
+    psend[...] = part[1 - core].astype(BF)
+    last_swap = remote(psend, precv, 22, 22, {"seq": mate})
+    last_swap.start()
+    base = hidden_buf[...].astype(F32) + part[core]
+    last_swap.wait_recv()
+    out_ref[...] = (base + precv[...].astype(F32)).astype(BF)
+
+    for copy in [swap, exchange, last_swap] + zcopies + heads + forwards + returns:
+        copy.wait_send()
+    for k in range(16):
+        target, copy = weight_copy(k)
+
+        @pl.when(target != me)
+        def _():
+            copy.wait_send()
+
+
+def call(length, samples, shard, first, middle, last, gain, proj, bias, attn_gain):
     vmem = pl.BlockSpec(memory_space=pltpu.VMEM)
     hbm = pl.BlockSpec(memory_space=pl.ANY)
+    rows, block = samples.shape
     width = proj.shape[1]
     return pl.pallas_call(
-        conv_kernel,
-        out_shape=[jax.ShapeDtypeStruct((FR, width), BF)] * 2,
+        kernel,
+        out_shape=jax.ShapeDtypeStruct((FR, width), BF),
         in_specs=[
-            pl.BlockSpec(memory_space=pltpu.SMEM), vmem, vmem, vmem, hbm, hbm, vmem, hbm, vmem, vmem,
+            pl.BlockSpec(memory_space=pltpu.SMEM), hbm, vmem, vmem, hbm, hbm, vmem, hbm, vmem, vmem,
         ],
-        out_specs=[vmem] * 2,
+        out_specs=vmem,
         scratch_shapes=[
-            pltpu.VMEM((FR + TAIL, 2688), BF),
+            pltpu.VMEM((rows, block), BF),
+            pltpu.VMEM((rows, block), BF),
+            pltpu.VMEM((FR + TAIL, block + 128), BF),
             pltpu.VMEM((33, FR, 2 * CH), BF),
             pltpu.VMEM((17, FR, 2 * CH), BF),
             pltpu.VMEM((9, FR, 2 * CH), BF),
@@ -212,69 +433,49 @@
             pltpu.VMEM(middle.shape, BF),
             pltpu.VMEM(last.shape, BF),
             pltpu.VMEM(proj.shape, BF),
-            pltpu.SemaphoreType.DMA((6,)),
+            pltpu.VMEM((4, 32, width), BF),
+            pltpu.VMEM((80, width), BF),
+            pltpu.VMEM((16, 80, width), BF),
+            pltpu.VMEM((2 * FR, width), BF),
+            pltpu.VMEM((FR, width), BF),
+            pltpu.VMEM((4, 240, 256), BF),
+            pltpu.VMEM((4, 240, 256), BF),
+            pltpu.VMEM((4, 4, 160, 256), BF),
+            pltpu.VMEM((4, 256, 80), BF),
+            pltpu.VMEM((4, 256, 1), F32),
+            pltpu.VMEM((4, 256, 1), F32),
+            pltpu.VMEM((4, 256, 80), F32),
+            pltpu.VMEM((4, 256, 128), BF),
+            pltpu.VMEM((4, 256, 128), BF),
+            pltpu.VMEM((2, FR, width), F32),
+            pltpu.VMEM((FR, width), BF),
+            pltpu.VMEM((FR, width), BF),
+            pltpu.SemaphoreType.DMA((10,)),
+            pltpu.SemaphoreType.DMA((48,)),
+            pltpu.SemaphoreType.DMA((48,)),
         ],
-        compiler_params=pltpu.CompilerParams(vmem_limit_bytes=56 << 20),
+        compiler_params=pltpu.CompilerParams(
+            vmem_limit_bytes=60 << 20, collective_id=0, has_side_effects=True
+        ),
         cost_estimate=pl.CostEstimate(
-            flops=16 * 10**9, bytes_accessed=14 * 10**6, transcendentals=9 * 10**6
+            flops=20 * 10**9, bytes_accessed=20 * 10**6, transcendentals=13 * 10**6
         ),
-        name="conv_stack",
+        name="encoder",
     )(
-        meta, own, arr, first, middle, last, gain.reshape(1, -1), proj, bias.reshape(1, -1),
-        attn_gain.reshape(1, -1),
+        length, samples, shard, first, middle, last, gain.reshape(1, -1), proj,
+        bias.reshape(1, -1), attn_gain.reshape(1, -1),
     )
-
-
-def partner(value, axis):
-    pairs = [(source, source ^ 1) for source in range(lax.axis_size(axis))]
-    return lax.ppermute(value, axis, pairs)
 
 
 def body(
     group_samples, group_lengths, group_offsets, conv_first, conv_middle, conv_last,
     feat_gain, proj_weight, proj_bias, attn_gain, attn_weight,
 ):
-    panels = lax.all_gather(attn_weight, ("dp", "seq"), axis=1, tiled=True)
-    inner_width = panels.shape[1] // 4
-    head_size = inner_width // HEADS
-    is_odd = lax.axis_index("seq") % 2
-    samples = group_samples[0, 0]
-    rows = samples.shape[0]
-    length = group_lengths[0, 0]
-    even_len = jnp.where(is_odd == 1, 2 * FR - length, length)
-    outgoing = jnp.where(is_odd == 1, samples[:SWAP], samples[rows - SWAP :])
-    arrived = partner(outgoing, "seq")
-    meta = jnp.stack([is_odd, even_len]).astype(jnp.int32)
-    hidden_x, normed_x = conv_call(
-        meta, samples, arrived, conv_first, conv_middle, conv_last, feat_gain, proj_weight,
-        proj_bias, attn_gain,
+    shard = jnp.pad(attn_weight.T, ((0, 12), (0, 0)))
+    encoded = call(
+        group_lengths, group_samples[0, 0], shard, conv_first, conv_middle, conv_last,
+        feat_gain, proj_weight, proj_bias, attn_gain,
     )
-    projected = jnp.dot(
-        normed_x, panels[:, : 3 * inner_width], preferred_element_type=F32
-    ).astype(BF)
-    queries = projected[:, :inner_width]
-    keys_local = projected[:, inner_width : 2 * inner_width]
-    values_local = projected[:, 2 * inner_width :]
-    scale = 1.0 / jnp.sqrt(jnp.float32(head_size))
-    queries3 = queries.reshape(FR, HEADS, head_size)
-    key_piece = lax.all_gather(keys_local, "seq", axis=0, tiled=True).reshape(-1, HEADS, head_size)
-    value_piece = lax.all_gather(values_local, "seq", axis=0, tiled=True).reshape(
-        -1, HEADS, head_size
-    )
-    scores = (
-        jnp.einsum("qhd,khd->hqk", queries3, key_piece, preferred_element_type=F32) * scale
-    )
-    peak = jnp.max(scores, axis=-1)
-    expo = jnp.exp(scores - peak[:, :, None])
-    total = jnp.sum(expo, axis=-1)
-    accum = jnp.einsum("hqk,khd->hqd", expo.astype(BF), value_piece, preferred_element_type=F32)
-    mixed = (
-        jnp.transpose(accum / total[:, :, None], (1, 0, 2)).reshape(FR, inner_width).astype(BF)
-    )
-    out_proj = lax.dot_general(
-        mixed, panels[:, 3 * inner_width :], (((1,), (1,)), ((), ())), preferred_element_type=F32
-    )
-    encoded = (hidden_x.astype(F32) + out_proj).astype(BF)
     return encoded.reshape(1, FR, -1)
 
 

time: 222 us -> 124 us (0.56)
  the two profiles are of different devices: /device:TPU:1 before, /device:TPU:3 now
where the time goes in v1:
time: 124 us
  Pallas kernels  117 us (94%)
  local copies, waits for them, and re-layouts  5.77 us (5%)
    pallas_call x1, Pallas kernels, call(): pl.pallas_call(kernel, out_shape=jax.ShapeDtypeStruct((FR, width), BF), i...  117 us

profile of v1, /device:TPU:3, one launch (start us, length us, event | category | flops | bytes accessed | tf_op | source)
XLA Modules:
  0.0 123.8 jit_solution(8578041098411383145)
XLA Ops:
  0.7 1.3 %reshape.13.bias = f32[1,1280]{1,0:T(1,128)} reshape(f32[1280]{0:T(1024)} %param.18) | data formatting | bytes 10240 | tf_op jit(solution)/shard_map/reshape | solution.py:466
  1.9 1.3 %reshape.14.attn_gain = f32[1,1280]{1,0:T(1,128)} reshape(f32[1280]{0:T(1024)} %param.19) | data formatting | bytes 10240 | tf_op jit(solution)/shard_map/reshape | solution.py:466
  3.2 1.5 %pad.4.shard = bf16[32,1280]{1,0:T(8,128)(2,1)} pad(bf16[20,1280]{1,0:T(8,128)(2,1)} %bitcast.5, bf16[]{:T(256)} %constant.2.clone.1), padding=0_12x0_0 | pad | bytes 133122 | tf_op jit(solution)/shard_map/jit(_pad)/pad | solution.py:474
  4.7 117.3 %encoder.1 = bf16[128,1280]{1,0:T(8,128)(2,1)} custom-call(s32[1,1]{1,0:T(1,128)S(6)} %copy.12.length, bf16[193,2560]{1,0:T(8,128)(2,1)} %bitcast.6, bf16[32,1280]{1,0:T(8,128)(2,1)} %pad.4.shard, bf16[80,512]{1,0:T(8,128)(2,1)} %first.1, bf16[4,1536,512]{2,1,0:T(8,128)(2,1)} %middle_hbm.1, bf16[2,1024,512]{2,1,0:T(8,128)(2,1)} %last_hbm.1, ...), custom_call_target="tpu_custom_call" | custom-call | flops 20000000000 | bytes 20000000 | tf_op jit(solution)/shard_map/encoder/pallas_call | solution.py:410
  122.1 1.7 %copy.13 = bf16[1,128,1280]{2,1,0:T(8,128)(2,1)} copy(bf16[1,128,1280]{2,1,0:T(8,128)(2,1)} %bitcast.4) | data formatting | bytes 655360

commit v2 on v1

--- a/solution.py
+++ b/solution.py
@@ -49,7 +49,7 @@
     length, samples_hbm, shard, first, middle_hbm, last_hbm, gain, proj_hbm, bias, attn_gain,
     out_ref,
     own, arr, x, a1, a2, a3, a4, a5, a6, t1, t2, t3, t4, acc0, acc1, middle, last, proj,
-    zbuf, wblk, wbuf, normed2, hidden_buf, ysend, qkv, kvbuf, qs, peak, total, accum,
+    zbuf, wblk, wbuf, normed2, hidden_buf, ysend, qkv, kvbuf, qs, peak, accum,
     mout, mbuf, part, psend, precv, sems, send_sems, recv_sems,
 ):
     me = lax.axis_index("seq")
@@ -76,20 +76,16 @@
     def greet(device):
         pl.semaphore_signal(barrier, inc=1, device_id=device, device_id_type=MESH)
 
+    def at(px, py, pc):
+        return {"seq": (px * 4 + py) * 2 + pc}
+
     greet({"seq": mate})
     for d in range(1, 4):
         greet({"dp": (night + d) % 4})
-        greet({"seq": place((ha + d) % 4, qb)})
-        greet({"seq": place(ha, (qb + d) % 4)})
-    for k in range(16):
-        source = 16 * core + k
-
-        @pl.when(source != me)
-        def _():
-            greet({"seq": source})
-
-    in_set = jnp.where(half == core, 1, 0)
-    pl.semaphore_wait(barrier, 26 - in_set)
+        for pc in range(2):
+            greet(at((cx + d) % 4, cy, pc))
+            greet(at(cx, (cy + d) % 4, pc))
+    pl.semaphore_wait(barrier, 16)
 
     swap = remote(samples_hbm, arr, 20, 20, {"seq": mate})
     swap.start()
@@ -136,27 +132,110 @@
     zown.wait()
     for copy in zcopies:
         copy.wait_recv()
-    cr = lax.broadcasted_iota(jnp.int32, (80, 128), 0)
-    cc = lax.broadcasted_iota(jnp.int32, (80, 128), 1)
-    wblk[...] = dot(
-        onehot(cc == 32 * (cr // 20) + cr % 20), zbuf[...].reshape(128, zbuf.shape[2])
-    ).astype(BF)
+    cr = lax.broadcasted_iota(jnp.int32, (80, 20), 0)
+    cc = lax.broadcasted_iota(jnp.int32, (80, 20), 1)
+    packed = sum(dot(onehot(cr == cc + 20 * p), zbuf[p]) for p in range(4)).astype(BF)
+    wide = packed.shape[1] // 2
+    wblk[0] = packed[:, :wide]
+    wblk[1] = packed[:, wide:]
     slot = me - 16 * half
-
-    def weight_copy(k):
-        target = ((chip + k) % 16) * 2 + half
-        return target, remote(wblk, wbuf.at[slot], k, slot, {"seq": target})
-
-    for k in range(16):
-        target, copy = weight_copy(k)
-
-        @pl.when(target != me)
+    first_hops = []
+    for d in range(4):
+        ty, tx = (cy + d) % 4, (cx + d) % 4
+        first_hops.append((
+            at(cx, ty, half),
+            remote(wblk.at[0], wbuf.at[0, slot], 48 + d, 48 + slot % 8, at(cx, ty, half)),
+        ))
+        first_hops.append((
+            at(tx, cy, half),
+            remote(
+                wblk.at[1], wbuf.at[1, slot], 52 + d, 56 + (cx % 2) * 2 + core, at(tx, cy, half)
+            ),
+        ))
+    for target, copy in first_hops:
+
+        @pl.when(target["seq"] != me)
         def _():
             copy.start()
 
     @pl.when(half == core)
     def _():
-        wbuf[slot] = wblk[...]
+        wbuf[0, slot] = wblk[0]
+        wbuf[1, slot] = wblk[1]
+
+    row_slots = pl.ds(8 * (cx % 2), 8)
+    x_hops = [
+        remote(
+            wbuf.at[0, row_slots], wbuf.at[0, row_slots], 60 + d, 60 + cx % 2,
+            at((cx + d) % 4, cy, core),
+        )
+        for d in range(1, 4)
+    ]
+    y_hops = [
+        remote(
+            wbuf.at[1, pl.ds(8 * p + 2 * cy, 2)], wbuf.at[1, pl.ds(8 * p + 2 * cy, 2)],
+            64 + 2 * d + p, 64 + 2 * (4 - d) + p, at(cx, (cy + d) % 4, core),
+        )
+        for d in range(1, 4)
+        for p in range(2)
+    ]
+
+    def second_hops():
+        for k in range(8):
+
+            @pl.when((half == core) & (k != slot % 8))
+            def _():
+                remote(
+                    wblk.at[0], wbuf.at[0, 8 * (cx % 2) + k], 48, 48 + k, {"seq": mate}
+                ).wait_recv()
+
+        @pl.when(half == core)
+        def _():
+            for copy in x_hops:
+                copy.start()
+
+        for k in range(4):
+            from_x, from_core = 2 * core + k // 2, k % 2
+
+            @pl.when((from_x != cx) | (from_core != core))
+            def _():
+                remote(
+                    wblk.at[1], wbuf.at[1, 8 * (k // 2) + 2 * cy + from_core], 52, 56 + k,
+                    {"seq": mate},
+                ).wait_recv()
+
+        for copy in y_hops:
+            copy.start()
+
+    def weights_arrived():
+        for p in range(2):
+
+            @pl.when(2 * core + p != cx)
+            def _():
+                remote(
+                    wbuf.at[0, pl.ds(8 * p, 8)], wbuf.at[0, pl.ds(8 * p, 8)], 60, 60 + p,
+                    {"seq": mate},
+                ).wait_recv()
+
+        for d in range(1, 4):
+            for p in range(2):
+                block = wbuf.at[1, pl.ds(8 * p + 2 * ((cy + d) % 4), 2)]
+                remote(block, block, 64, 64 + 2 * d + p, {"seq": mate}).wait_recv()
+
+    def weights_sent():
+        for target, copy in first_hops:
+
+            @pl.when(target["seq"] != me)
+            def _():
+                copy.wait_send()
+
+        @pl.when(half == core)
+        def _():
+            for copy in x_hops:
+                copy.wait_send()
+
+        for copy in y_hops:
+            copy.wait_send()
 
     swap.wait_recv()
     pick_own, pick_arr = picks(own_rows, 0, 0), picks(own_rows, own_rows, 0)
@@ -200,7 +279,9 @@
         layer_one(2 * i + 1, acc1, 1, i)
         return carry
 
-    lax.fori_loop(0, 8, one_step, 0)
+    lax.fori_loop(0, 4, one_step, 0)
+    second_hops()
+    lax.fori_loop(4, 8, one_step, 0)
     close(a1, t1)
 
     def three_taps(ain, start, count, rows, layer, acc):
@@ -271,13 +352,13 @@
     mine = normed2.at[pl.ds(pl.multiple_of(core * FR, FR), FR)]
     exchange = remote(mine, mine, 21, 21, {"seq": mate})
     exchange.start()
-    for k in range(16):
-
-        @pl.when(16 * core + k != me)
-        def _():
-            remote(wblk, wbuf.at[k], 0, k, {"seq": mate}).wait_recv()
-
+    weights_arrived()
     exchange.wait_recv()
+
+    def head_weights(h):
+        return jnp.concatenate(
+            [wbuf[p, pl.ds(4 * h, 4)].reshape(320, wbuf.shape[3]) for p in range(2)], axis=1
+        )
 
     yr = lax.broadcasted_iota(jnp.int32, (320, 1), 0)
     row_scale = jnp.where(yr % 80 < 20, SCALE, 1.0).astype(F32)
@@ -286,8 +367,7 @@
     regroup = onehot(pc == 80 * ((pr % 80) // 20) + 20 * (pr // 80) + pr % 20)
 
     def project(h, carry):
-        w = wbuf[pl.ds(4 * h, 4)].reshape(320, wbuf.shape[2])
-        y = lax.dot_general(w, normed2[...], NT, preferred_element_type=F32)
+        y = lax.dot_general(head_weights(h), normed2[...], NT, preferred_element_type=F32)
         ysend[h] = dot(regroup, (y * row_scale).astype(BF)).astype(BF)
         return carry
 
@@ -325,6 +405,10 @@
     for i in range(4):
         qs[i] = jnp.transpose(qkv[i, :80, :].astype(F32)).astype(BF)
 
+    def masses(values):
+        ones = jnp.ones((16, values.shape[1]), BF)
+        return jnp.concatenate([values, ones], axis=0)
+
     def attend(keys, values, is_first):
         def step(i, carry):
             s = dot(qs[i], keys)
@@ -332,18 +416,15 @@
             if not is_first:
                 top = jnp.maximum(top, peak[i])
             p = jnp.exp2(s - top)
-            mass = jnp.sum(p, axis=-1, keepdims=True)
-            o = lax.dot_general(p.astype(BF), values, NT, preferred_element_type=F32)
+            o = lax.dot_general(p.astype(BF), masses(values), NT, preferred_element_type=F32)
             if not is_first:
                 fade = jnp.exp2(peak[i] - top)
-                mass = mass + total[i] * fade
                 o = o + accum[i] * fade
             peak[i] = top
-            total[i] = mass
             accum[i] = o
             return carry
 
-        lax.fori_loop(0, 4, step, 0)
+        lax.fori_loop(0, 2, lambda i, c: step(2 * i + 1, step(2 * i, c)), 0)
 
     attend(
         jnp.concatenate([qkv[i, 80:160, :] for i in range(4)], axis=1),
@@ -363,7 +444,7 @@
             False,
         )
     for i in range(4):
-        mout[i, :, :80] = (accum[i] / total[i]).astype(BF)
+        mout[i, :, :80] = (accum[i, :, :80] / accum[i, :, 80:81]).astype(BF)
     returns = []
     for d in range(1, 4):
         to = (ha + d) % 4
@@ -382,7 +463,7 @@
     sums = None
     for h in range(4):
         wide = dot(mbuf[h], spread).astype(BF)
-        term = dot(wide, wbuf[4 * h : 4 * h + 4].reshape(320, wbuf.shape[2]))
+        term = dot(wide, head_weights(h))
         sums = term if sums is None else sums + term
     part[...] = sums.reshape(2, FR, sums.shape[1])
     psend[...] = part[1 - core].astype(BF)
@@ -394,12 +475,7 @@
 
     for copy in [swap, exchange, last_swap] + zcopies + heads + forwards + returns:
         copy.wait_send()
-    for k in range(16):
-        target, copy = weight_copy(k)
-
-        @pl.when(target != me)
-        def _():
-            copy.wait_send()
+    weights_sent()
 
 
 def call(length, samples, shard, first, middle, last, gain, proj, bias, attn_gain):
@@ -411,7 +487,7 @@
         kernel,
         out_shape=jax.ShapeDtypeStruct((FR, width), BF),
         in_specs=[
-            pl.BlockSpec(memory_space=pltpu.SMEM), hbm, vmem, vmem, hbm, hbm, vmem, hbm, vmem, vmem,
+            pl.BlockSpec(memory_space=pltpu.SMEM), hbm, hbm, vmem, hbm, hbm, vmem, hbm, vmem, vmem,
         ],
         out_specs=vmem,
         scratch_shapes=[
@@ -433,9 +509,9 @@
             pltpu.VMEM(middle.shape, BF),
             pltpu.VMEM(last.shape, BF),
             pltpu.VMEM(proj.shape, BF),
-            pltpu.VMEM((4, 32, width), BF),
-            pltpu.VMEM((80, width), BF),
-            pltpu.VMEM((16, 80, width), BF),
+            pltpu.VMEM((4, 20, width), BF),
+            pltpu.VMEM((2, 80, width // 2), BF),
+            pltpu.VMEM((2, 16, 80, width // 2), BF),
             pltpu.VMEM((2 * FR, width), BF),
             pltpu.VMEM((FR, width), BF),
             pltpu.VMEM((4, 240, 256), BF),
@@ -443,16 +519,15 @@
             pltpu.VMEM((4, 4, 160, 256), BF),
             pltpu.VMEM((4, 256, 80), BF),
             pltpu.VMEM((4, 256, 1), F32),
-            pltpu.VMEM((4, 256, 1), F32),
-            pltpu.VMEM((4, 256, 80), F32),
+            pltpu.VMEM((4, 256, 96), F32),
             pltpu.VMEM((4, 256, 128), BF),
             pltpu.VMEM((4, 256, 128), BF),
             pltpu.VMEM((2, FR, width), F32),
             pltpu.VMEM((FR, width), BF),
             pltpu.VMEM((FR, width), BF),
             pltpu.SemaphoreType.DMA((10,)),
-            pltpu.SemaphoreType.DMA((48,)),
-            pltpu.SemaphoreType.DMA((48,)),
+            pltpu.SemaphoreType.DMA((72,)),
+            pltpu.SemaphoreType.DMA((72,)),
         ],
         compiler_params=pltpu.CompilerParams(
             vmem_limit_bytes=60 << 20, collective_id=0, has_side_effects=True
@@ -462,8 +537,8 @@
         ),
         name="encoder",
     )(
-        length, samples, shard, first, middle, last, gain.reshape(1, -1), proj,
-        bias.reshape(1, -1), attn_gain.reshape(1, -1),
+        length, samples, shard, first, middle, last, gain, proj, bias,
+        attn_gain,
     )
 
 
@@ -471,9 +546,8 @@
     group_samples, group_lengths, group_offsets, conv_first, conv_middle, conv_last,
     feat_gain, proj_weight, proj_bias, attn_gain, attn_weight,
 ):
-    shard = jnp.pad(attn_weight.T, ((0, 12), (0, 0)))
     encoded = call(
-        group_lengths, group_samples[0, 0], shard, conv_first, conv_middle, conv_last,
+        group_lengths, group_samples[0, 0], attn_weight.T, conv_first, conv_middle, conv_last,
         feat_gain, proj_weight, proj_bias, attn_gain,
     )
     return encoded.reshape(1, FR, -1)

time: 124 us -> 86.3 us (0.70)
  the two profiles are of different devices: /device:TPU:3 before, /device:TPU:1 now
where the time goes in v2:
time: 86.3 us; the launch traced here: 85.9 us
  Pallas kernels  83.6 us (97%)
  local copies, waits for them, and re-layouts  1.72 us (2%)
    pallas_call x1, Pallas kernels, call(): pl.pallas_call(kernel, out_shape=jax.ShapeDtypeStruct((FR, width), BF), i...  83.6 us

profile of v2, /device:TPU:1, one launch (start us, length us, event | category | flops | bytes accessed | tf_op | source)
XLA Modules:
  0.0 85.9 jit_solution(4177187205637025391)
XLA Ops:
  0.7 83.6 %encoder.1 = bf16[128,1280]{1,0:T(8,128)(2,1)} custom-call(s32[1,1]{1,0:T(1,128)S(6)} %copy.12.length, bf16[193,2560]{1,0:T(8,128)(2,1)} %bitcast.4, bf16[20,1280]{1,0:T(8,128)(2,1)} %bitcast.5, bf16[80,512]{1,0:T(8,128)(2,1)} %first.1, bf16[4,1536,512]{2,1,0:T(8,128)(2,1)} %middle_hbm.1, bf16[2,1024,512]{2,1,0:T(8,128)(2,1)} %last_hbm.1, f32[512]{0:T(512)} %gain.1, ...), custom_call_target="tpu_custom_call" | custom-call | flops 20000000000 | bytes 20000000 | tf_op jit(solution)/shard_map/encoder/pallas_call | solution.py:486
  84.2 1.7 %copy.13 = bf16[1,128,1280]{2,1,0:T(8,128)(2,1)} copy(bf16[1,128,1280]{2,1,0:T(8,128)(2,1)} %bitcast.3) | data formatting | bytes 655360

commit v3 on v2

--- a/solution.py
+++ b/solution.py
@@ -49,8 +49,8 @@
     length, samples_hbm, shard, first, middle_hbm, last_hbm, gain, proj_hbm, bias, attn_gain,
     out_ref,
     own, arr, x, a1, a2, a3, a4, a5, a6, t1, t2, t3, t4, acc0, acc1, middle, last, proj,
-    zbuf, wblk, wbuf, normed2, hidden_buf, ysend, qkv, kvbuf, qs, peak, accum,
-    mout, mbuf, part, psend, precv, sems, send_sems, recv_sems,
+    shard_buf, zbuf, wblk, wbuf, normed2, hidden_buf, ysend, qkv, kvbuf, qs, peak, accum,
+    mout, mbuf, widen, psend, precv, sems, send_sems, recv_sems,
 ):
     me = lax.axis_index("seq")
     night = lax.axis_index("dp")
@@ -85,20 +85,10 @@
         for pc in range(2):
             greet(at((cx + d) % 4, cy, pc))
             greet(at(cx, (cy + d) % 4, pc))
-    pl.semaphore_wait(barrier, 16)
-
-    swap = remote(samples_hbm, arr, 20, 20, {"seq": mate})
-    swap.start()
-    zcopies = [
-        remote(shard, zbuf.at[night], 16 + d, 16 + (4 - d) % 4, {"dp": (night + d) % 4})
-        for d in range(1, 4)
-    ]
-    for copy in zcopies:
-        copy.start()
     own_copy = pltpu.make_async_copy(samples_hbm, own, sems.at[6])
     own_copy.start()
-    zown = pltpu.make_async_copy(shard, zbuf.at[night], sems.at[7])
-    zown.start()
+    shard_copy = pltpu.make_async_copy(shard, shard_buf, sems.at[7])
+    shard_copy.start()
     copies = [
         pltpu.make_async_copy(middle_hbm.at[l], middle.at[l], sems.at[l]) for l in range(4)
     ]
@@ -128,16 +118,34 @@
         )
         return onehot(src == col)
 
+    shard_copy.wait()
+    gr = lax.broadcasted_iota(jnp.int32, (32, 20), 0)
+    gc = lax.broadcasted_iota(jnp.int32, (32, 20), 1)
+    zbuf[night] = dot(onehot(gr == gc), shard_buf[...]).astype(BF)
     own_copy.wait()
-    zown.wait()
+    pick_own = picks(own_rows, 0, 0)
+    for c in range(0, 2560, 512):
+        x[:, c : c + 512] = dot(pick_own, own[:, c : c + 512]).astype(BF)
+    x[:, 2560:2688] = dot(picks(own_rows, 0, 1), own[:, :128]).astype(BF)
+    for h in range(4):
+        lanes_h = lax.broadcasted_iota(jnp.int32, (128, widen.shape[1]), 1)
+        rows_h = lax.broadcasted_iota(jnp.int32, (128, widen.shape[1]), 0)
+        widen[128 * h : 128 * h + 128, :] = onehot(
+            (lanes_h == 320 * h + 80 * (rows_h // 20) + 60 + rows_h % 20) & (rows_h < 80)
+        )
+    mout[...] = jnp.zeros_like(mout)
+
+    pl.semaphore_wait(barrier, 16)
+    mine_z = zbuf.at[night]
+    zcopies = [
+        remote(mine_z, mine_z, 16 + d, 16 + (4 - d) % 4, {"dp": (night + d) % 4})
+        for d in range(1, 4)
+    ]
     for copy in zcopies:
-        copy.wait_recv()
-    cr = lax.broadcasted_iota(jnp.int32, (80, 20), 0)
-    cc = lax.broadcasted_iota(jnp.int32, (80, 20), 1)
-    packed = sum(dot(onehot(cr == cc + 20 * p), zbuf[p]) for p in range(4)).astype(BF)
-    wide = packed.shape[1] // 2
-    wblk[0] = packed[:, :wide]
-    wblk[1] = packed[:, wide:]
+        copy.start()
+    swap = remote(samples_hbm, arr, 20, 20, {"seq": mate})
+    swap.start()
+
     slot = me - 16 * half
     first_hops = []
     for d in range(4):
@@ -152,16 +160,27 @@
                 wblk.at[1], wbuf.at[1, slot], 52 + d, 56 + (cx % 2) * 2 + core, at(tx, cy, half)
             ),
         ))
-    for target, copy in first_hops:
-
-        @pl.when(target["seq"] != me)
+    def start_weights():
+        for copy in zcopies:
+            copy.wait_recv()
+        cr = lax.broadcasted_iota(jnp.int32, (80, 128), 0)
+        cc = lax.broadcasted_iota(jnp.int32, (80, 128), 1)
+        packed = dot(
+            onehot(cc == 32 * (cr // 20) + cr % 20), zbuf[...].reshape(128, zbuf.shape[2])
+        ).astype(BF)
+        wide = packed.shape[1] // 2
+        wblk[0] = packed[:, :wide]
+        wblk[1] = packed[:, wide:]
+        for target, copy in first_hops:
+
+            @pl.when(target["seq"] != me)
+            def _():
+                copy.start()
+
+        @pl.when(half == core)
         def _():
-            copy.start()
-
-    @pl.when(half == core)
-    def _():
-        wbuf[0, slot] = wblk[0]
-        wbuf[1, slot] = wblk[1]
+            wbuf[0, slot] = wblk[0]
+            wbuf[1, slot] = wblk[1]
 
     row_slots = pl.ds(8 * (cx % 2), 8)
     x_hops = [
@@ -238,14 +257,10 @@
             copy.wait_send()
 
     swap.wait_recv()
-    pick_own, pick_arr = picks(own_rows, 0, 0), picks(own_rows, own_rows, 0)
+    pick_arr = picks(own_rows, own_rows, 0)
     for c in range(0, 2560, 512):
-        x[:, c : c + 512] = (
-            dot(pick_own, own[:, c : c + 512]) + dot(pick_arr, arr[:, c : c + 512])
-        ).astype(BF)
-    x[:, 2560:2688] = (
-        dot(picks(own_rows, 0, 1), own[:, :128]) + dot(picks(own_rows, own_rows, 1), arr[:, :128])
-    ).astype(BF)
+        x[:, c : c + 512] += dot(pick_arr, arr[:, c : c + 512]).astype(BF)
+    x[:, 2560:2688] += dot(picks(own_rows, own_rows, 1), arr[:, :128]).astype(BF)
 
     nr = lax.broadcasted_iota(jnp.int32, (FR, FR + TAIL), 0)
     nc = lax.broadcasted_iota(jnp.int32, (FR, FR + TAIL), 1)
@@ -279,9 +294,11 @@
         layer_one(2 * i + 1, acc1, 1, i)
         return carry
 
-    lax.fori_loop(0, 4, one_step, 0)
+    lax.fori_loop(0, 2, one_step, 0)
+    start_weights()
+    lax.fori_loop(2, 5, one_step, 0)
     second_hops()
-    lax.fori_loop(4, 8, one_step, 0)
+    lax.fori_loop(5, 8, one_step, 0)
     close(a1, t1)
 
     def three_taps(ain, start, count, rows, layer, acc):
@@ -371,37 +388,33 @@
         ysend[h] = dot(regroup, (y * row_scale).astype(BF)).astype(BF)
         return carry
 
-    lax.fori_loop(0, 4, project, 0)
-
-    heads = []
-    for d in range(1, 4):
-        to = (ha + d) % 4
-        heads.append(
-            remote(ysend.at[to], qkv.at[ha], 24 + d, 24 + (4 - d) % 4, {"seq": place(to, qb)})
-        )
-        heads[-1].start()
-    keep = pltpu.make_async_copy(ysend.at[ha], qkv.at[ha], sems.at[8])
-    keep.start()
-
     forwards = []
 
-    def forward(d):
-        src = qkv.at[(ha + d) % 4, pl.ds(80, 160)]
+    def forward(d, block):
         for e in range(1, 4):
             copy = remote(
-                src, kvbuf.at[qb, (ha + d) % 4], 28 + 4 * d + e, 28 + 4 * d + (4 - e) % 4,
-                {"seq": place(ha, (qb + e) % 4)},
+                block.at[pl.ds(80, 160)], kvbuf.at[qb, (ha + d) % 4],
+                28 + 4 * d + e, 28 + 4 * d + (4 - e) % 4, {"seq": place(ha, (qb + e) % 4)},
             )
             copy.start()
             forwards.append(copy)
 
-    keep.wait()
-    forward(0)
+    heads = []
+    for d in (0, 1, 3, 2):
+        to = (ha + d) % 4
+        project(to, 0)
+        if d == 0:
+            forward(0, ysend.at[ha])
+            continue
+        heads.append(
+            remote(ysend.at[to], qkv.at[ha], 24 + d, 24 + (4 - d) % 4, {"seq": place(to, qb)})
+        )
+        heads[-1].start()
+    qkv[ha] = ysend[ha]
     for d in (3, 1, 2):
         remote(ysend.at[0], qkv.at[(ha + d) % 4], 24, 24 + d, {"seq": mate}).wait_recv()
-        forward(d)
-
-    mout[...] = jnp.zeros_like(mout)
+        forward(d, qkv.at[(ha + d) % 4])
+
     for i in range(4):
         qs[i] = jnp.transpose(qkv[i, :80, :].astype(F32)).astype(BF)
 
@@ -409,7 +422,7 @@
         ones = jnp.ones((16, values.shape[1]), BF)
         return jnp.concatenate([values, ones], axis=0)
 
-    def attend(keys, values, is_first):
+    def attend(keys, values, is_first, finish=None):
         def step(i, carry):
             s = dot(qs[i], keys)
             top = jnp.max(s, axis=-1, keepdims=True)
@@ -424,52 +437,57 @@
             accum[i] = o
             return carry
 
-        lax.fori_loop(0, 2, lambda i, c: step(2 * i + 1, step(2 * i, c)), 0)
-
-    attend(
-        jnp.concatenate([qkv[i, 80:160, :] for i in range(4)], axis=1),
-        jnp.concatenate([qkv[i, 160:240, :] for i in range(4)], axis=1),
-        True,
-    )
-    for e in (1, 3, 2):
-        b = (qb + e) % 4
-        for d in range(4):
+        if finish is None:
+            lax.fori_loop(0, 2, lambda i, c: step(2 * i + 1, step(2 * i, c)), 0)
+        else:
+            for d in (1, 2, 3, 0):
+                step((ha + d) % 4, 0)
+                finish(d)
+
+    returns = []
+    keep2 = pltpu.make_async_copy(mout.at[ha], mbuf.at[ha], sems.at[9])
+
+    def give_back(d):
+        to = (ha + d) % 4
+        mout[to, :, :80] = (accum[to, :, :80] / accum[to, :, 80:81]).astype(BF)
+        if d == 0:
+            keep2.start()
+        else:
+            returns.append(
+                remote(mout.at[to], mbuf.at[ha], 44 + d, 44 + (4 - d) % 4, {"seq": place(to, qb)})
+            )
+            returns[-1].start()
+
+    for d in (0, 3, 1, 2):
+        a = (ha + d) % 4
+        for e in range(1, 4):
             remote(
-                qkv.at[0, pl.ds(80, 160)], kvbuf.at[b, (ha + d) % 4], 28, 28 + 4 * d + e,
+                qkv.at[0, pl.ds(80, 160)], kvbuf.at[(qb + e) % 4, a], 28, 28 + 4 * d + e,
                 {"seq": mate},
             ).wait_recv()
+        blocks = [qkv[a, 80:, :]] + [kvbuf[(qb + e) % 4, a] for e in range(1, 4)]
         attend(
-            jnp.concatenate([kvbuf[b, i, :80, :] for i in range(4)], axis=1),
-            jnp.concatenate([kvbuf[b, i, 80:, :] for i in range(4)], axis=1),
-            False,
-        )
-    for i in range(4):
-        mout[i, :, :80] = (accum[i, :, :80] / accum[i, :, 80:81]).astype(BF)
-    returns = []
-    for d in range(1, 4):
-        to = (ha + d) % 4
-        returns.append(
-            remote(mout.at[to], mbuf.at[ha], 44 + d, 44 + (4 - d) % 4, {"seq": place(to, qb)})
-        )
-        returns[-1].start()
-    keep2 = pltpu.make_async_copy(mout.at[ha], mbuf.at[ha], sems.at[9])
-    keep2.start()
-    er = lax.broadcasted_iota(jnp.int32, (128, 320), 0)
-    ec = lax.broadcasted_iota(jnp.int32, (128, 320), 1)
-    spread = onehot((ec == 80 * (er // 20) + 60 + er % 20) & (er < 80))
+            jnp.concatenate([block[:80] for block in blocks], axis=1),
+            jnp.concatenate([block[80:] for block in blocks], axis=1),
+            d == 0,
+            give_back if d == 2 else None,
+        )
     keep2.wait()
     for d in range(1, 4):
         remote(mout.at[0], mbuf.at[(ha + d) % 4], 44, 44 + d, {"seq": mate}).wait_recv()
-    sums = None
-    for h in range(4):
-        wide = dot(mbuf[h], spread).astype(BF)
-        term = dot(wide, head_weights(h))
-        sums = term if sums is None else sums + term
-    part[...] = sums.reshape(2, FR, sums.shape[1])
-    psend[...] = part[1 - core].astype(BF)
+
+    def output(rows_of):
+        rows = pl.ds(pl.multiple_of(rows_of * FR, FR), FR)
+        mixed = jnp.concatenate([mbuf[h, rows, :] for h in range(4)], axis=1)
+        wide = dot(mixed, widen[...]).astype(BF)
+        return jnp.concatenate(
+            [dot(wide, wbuf[p].reshape(1280, wbuf.shape[3])) for p in range(2)], axis=1
+        )
+
+    psend[...] = output(1 - core).astype(BF)
     last_swap = remote(psend, precv, 22, 22, {"seq": mate})
     last_swap.start()
-    base = hidden_buf[...].astype(F32) + part[core]
+    base = hidden_buf[...].astype(F32) + output(core)
     last_swap.wait_recv()
     out_ref[...] = (base + precv[...].astype(F32)).astype(BF)
 
@@ -509,7 +527,8 @@
             pltpu.VMEM(middle.shape, BF),
             pltpu.VMEM(last.shape, BF),
             pltpu.VMEM(proj.shape, BF),
-            pltpu.VMEM((4, 20, width), BF),
+            pltpu.VMEM((20, width), BF),
+            pltpu.VMEM((4, 32, width), BF),
             pltpu.VMEM((2, 80, width // 2), BF),
             pltpu.VMEM((2, 16, 80, width // 2), BF),
             pltpu.VMEM((2 * FR, width), BF),
@@ -522,7 +541,7 @@
             pltpu.VMEM((4, 256, 96), F32),
             pltpu.VMEM((4, 256, 128), BF),
             pltpu.VMEM((4, 256, 128), BF),
-            pltpu.VMEM((2, FR, width), F32),
+            pltpu.VMEM((512, width), BF),
             pltpu.VMEM((FR, width), BF),
             pltpu.VMEM((FR, width), BF),
             pltpu.SemaphoreType.DMA((10,)),

time: 86.3 us -> 78.1 us (0.905)
  Pallas kernels: 83.6 us -> 75.5 us
    pallas_call x1, Pallas kernels: 83.6 us -> 75.5 us  [call(): pl.pallas_call(kernel, out_shape=jax.ShapeDtypeStruct((FR, width), BF), i...]
where the time goes in v3:
time: 78.1 us; the launch traced here: 77.9 us
  Pallas kernels  75.5 us (97%)
  local copies, waits for them, and re-layouts  1.72 us (2%)
    pallas_call x1, Pallas kernels, call(): pl.pallas_call(kernel, out_shape=jax.ShapeDtypeStruct((FR, width), BF), i...  75.5 us
    unnamed x1, local copies, waits for them, and re-layouts  1.72 us

profile of v3, /device:TPU:1, one launch (start us, length us, event | category | flops | bytes accessed | tf_op | source)
XLA Modules:
  0.0 77.9 jit_solution(4190380198434885909)
XLA Ops:
  0.7 75.5 %encoder.1 = bf16[128,1280]{1,0:T(8,128)(2,1)} custom-call(s32[1,1]{1,0:T(1,128)S(6)} %copy.12.length, bf16[193,2560]{1,0:T(8,128)(2,1)} %bitcast.4, bf16[20,1280]{1,0:T(8,128)(2,1)} %bitcast.5, bf16[80,512]{1,0:T(8,128)(2,1)} %first.1, bf16[4,1536,512]{2,1,0:T(8,128)(2,1)} %middle_hbm.1, bf16[2,1024,512]{2,1,0:T(8,128)(2,1)} %last_hbm.1, f32[512]{0:T(512)} %gain.1, ...), custom_call_target="tpu_custom_call" | custom-call | flops 20000000000 | bytes 20000000 | tf_op jit(solution)/shard_map/encoder/pallas_call | solution.py:504
  76.2 1.7 %copy.13 = bf16[1,128,1280]{2,1,0:T(8,128)(2,1)} copy(bf16[1,128,1280]{2,1,0:T(8,128)(2,1)} %bitcast.3) | data formatting | bytes 655360

commit v4 on v3

--- a/solution.py
+++ b/solution.py
@@ -10,6 +10,7 @@
 FR = 128
 CH = 512
 TAIL = 16
+SWAP = 80
 BF = jnp.bfloat16
 F32 = jnp.float32
 SCALE = math.log2(math.e) / math.sqrt(80)
@@ -48,9 +49,9 @@
 def kernel(
     length, samples_hbm, shard, first, middle_hbm, last_hbm, gain, proj_hbm, bias, attn_gain,
     out_ref,
-    own, arr, x, a1, a2, a3, a4, a5, a6, t1, t2, t3, t4, acc0, acc1, middle, last, proj,
-    shard_buf, zbuf, wblk, wbuf, normed2, hidden_buf, ysend, qkv, kvbuf, qs, peak, accum,
-    mout, mbuf, widen, psend, precv, sems, send_sems, recv_sems,
+    own, outgoing, arr, x, a1, a2, a3, a4, a5, a6, t1, t2, t3, t4, acc0, acc1, middle, last, proj,
+    shifted, acc2, acc3, shard_buf, zbuf, wblk, wbuf, normed2, hidden_buf, ysend, qkv, kvbuf, qs, peak, accum,
+    mout, mbuf, out_weight, psend, precv, sems, send_sems, recv_sems,
 ):
     me = lax.axis_index("seq")
     night = lax.axis_index("dp")
@@ -106,7 +107,7 @@
     def source(r):
         even = jnp.where(r < even_len, r, own_rows + r - even_len)
         odd = jnp.where(
-            r + FR < even_len, own_rows + r + FR, r + FR - even_len
+            r + FR < even_len, own_rows + r + FR - (own_rows - SWAP), r + FR - even_len
         )
         return jnp.where(is_odd == 1, odd, even)
 
@@ -123,19 +124,14 @@
     gc = lax.broadcasted_iota(jnp.int32, (32, 20), 1)
     zbuf[night] = dot(onehot(gr == gc), shard_buf[...]).astype(BF)
     own_copy.wait()
-    pick_own = picks(own_rows, 0, 0)
+    sr = lax.broadcasted_iota(jnp.int32, (SWAP, own_rows), 0)
+    sc = lax.broadcasted_iota(jnp.int32, (SWAP, own_rows), 1)
+    pick_swap = onehot(sc == sr + jnp.where(core == 0, own_rows - SWAP, 0))
     for c in range(0, 2560, 512):
-        x[:, c : c + 512] = dot(pick_own, own[:, c : c + 512]).astype(BF)
-    x[:, 2560:2688] = dot(picks(own_rows, 0, 1), own[:, :128]).astype(BF)
-    for h in range(4):
-        lanes_h = lax.broadcasted_iota(jnp.int32, (128, widen.shape[1]), 1)
-        rows_h = lax.broadcasted_iota(jnp.int32, (128, widen.shape[1]), 0)
-        widen[128 * h : 128 * h + 128, :] = onehot(
-            (lanes_h == 320 * h + 80 * (rows_h // 20) + 60 + rows_h % 20) & (rows_h < 80)
-        )
-    mout[...] = jnp.zeros_like(mout)
-
+        outgoing[:, c : c + 512] = dot(pick_swap, own[:, c : c + 512]).astype(BF)
     pl.semaphore_wait(barrier, 16)
+    swap = remote(outgoing, arr, 20, 20, {"seq": mate})
+    swap.start()
     mine_z = zbuf.at[night]
     zcopies = [
         remote(mine_z, mine_z, 16 + d, 16 + (4 - d) % 4, {"dp": (night + d) % 4})
@@ -143,8 +139,19 @@
     ]
     for copy in zcopies:
         copy.start()
-    swap = remote(samples_hbm, arr, 20, 20, {"seq": mate})
-    swap.start()
+    pick_own = picks(own_rows, 0, 0)
+    for c in range(0, 2560, 512):
+        x[:, c : c + 512] = dot(pick_own, own[:, c : c + 512]).astype(BF)
+    x[:, 2560:2688] = dot(picks(own_rows, 0, 1), own[:, :128]).astype(BF)
+    mout[...] = jnp.zeros_like(mout)
+    er = lax.broadcasted_iota(jnp.int32, (256, 80), 0)
+    ec = lax.broadcasted_iota(jnp.int32, (256, 80), 1)
+
+    def shift(u, carry):
+        shifted[u] = dot(onehot(er == ec + lax.rem(40 * u, 128)), first[...]).astype(BF)
+        return carry
+
+    lax.fori_loop(0, 16, shift, 0)
 
     slot = me - 16 * half
     first_hops = []
@@ -188,14 +195,14 @@
             wbuf.at[0, row_slots], wbuf.at[0, row_slots], 60 + d, 60 + cx % 2,
             at((cx + d) % 4, cy, core),
         )
-        for d in range(1, 4)
+        for d in (2, 1, 3)
     ]
     y_hops = [
         remote(
             wbuf.at[1, pl.ds(8 * p + 2 * cy, 2)], wbuf.at[1, pl.ds(8 * p + 2 * cy, 2)],
             64 + 2 * d + p, 64 + 2 * (4 - d) + p, at(cx, (cy + d) % 4, core),
         )
-        for d in range(1, 4)
+        for d in (2, 1, 3)
         for p in range(2)
     ]
 
@@ -257,10 +264,10 @@
             copy.wait_send()
 
     swap.wait_recv()
-    pick_arr = picks(own_rows, own_rows, 0)
+    pick_arr = picks(SWAP, own_rows, 0)
     for c in range(0, 2560, 512):
         x[:, c : c + 512] += dot(pick_arr, arr[:, c : c + 512]).astype(BF)
-    x[:, 2560:2688] += dot(picks(own_rows, own_rows, 1), arr[:, :128]).astype(BF)
+    x[:, 2560:2688] += dot(picks(SWAP, own_rows, 1), arr[:, :128]).astype(BF)
 
     nr = lax.broadcasted_iota(jnp.int32, (FR, FR + TAIL), 0)
     nc = lax.broadcasted_iota(jnp.int32, (FR, FR + TAIL), 1)
@@ -274,12 +281,9 @@
     def layer_one(u, acc, parity, half):
         offset = lax.rem(40 * u, 128)
         base = pl.multiple_of(40 * u - offset, 128)
-        er = lax.broadcasted_iota(jnp.int32, (256, 80), 0)
-        ec = lax.broadcasted_iota(jnp.int32, (256, 80), 1)
-        weight = dot((er == ec + offset).astype(F32).astype(BF), first[...]).astype(BF)
         parts = [x[:FR, pl.ds(pl.multiple_of(base + 640 * b, 128), 256)] for b in range(4)]
         parts.append(x[FR:, pl.ds(base, 256)])
-        acc[...] = dot(jnp.concatenate(parts, axis=0), weight)
+        acc[...] = dot(jnp.concatenate(parts, axis=0), shifted[u])
 
         def out(r, n, val):
             if r < 4 * FR:
@@ -290,15 +294,14 @@
         settle(acc, 4 * FR + TAIL, 1e-5, out)
 
     def one_step(i, carry):
-        layer_one(2 * i, acc0, 0, i)
-        layer_one(2 * i + 1, acc1, 1, i)
+        for k, acc in enumerate((acc0, acc1, acc2, acc3)):
+            layer_one(4 * i + k, acc, k % 2, 2 * i + k // 2)
         return carry
 
-    lax.fori_loop(0, 2, one_step, 0)
+    lax.fori_loop(0, 1, one_step, 0)
     start_weights()
-    lax.fori_loop(2, 5, one_step, 0)
+    lax.fori_loop(1, 4, one_step, 0)
     second_hops()
-    lax.fori_loop(5, 8, one_step, 0)
     close(a1, t1)
 
     def three_taps(ain, start, count, rows, layer, acc):
@@ -331,16 +334,17 @@
         copies[index].wait()
 
         def step(i, carry):
-            main_chunk(ain, aout, index, 2 * i, acc0)
-            main_chunk(ain, aout, index, 2 * i + 1, acc1)
+            for k, acc in enumerate((acc0, acc1, acc2, acc3)):
+                main_chunk(ain, aout, index, 4 * i + k, acc)
             return carry
 
-        if chunks > 1:
-            lax.fori_loop(0, chunks // 2, step, 0)
+        if chunks >= 4:
+            lax.fori_loop(0, chunks // 4, step, 0)
         else:
-            main_chunk(ain, aout, index, 0, acc0)
+            for k in range(chunks):
+                main_chunk(ain, aout, index, k, (acc0, acc1)[k])
         if tail_count:
-            tail_chunk(tin, tout, index, tail_count, acc1)
+            tail_chunk(tin, tout, index, tail_count, acc2)
             close(aout, tout)
 
     layer(a1, a2, t1, t2, 0, 8, 7)
@@ -411,6 +415,11 @@
         )
         heads[-1].start()
     qkv[ha] = ysend[ha]
+    wr = lax.broadcasted_iota(jnp.int32, (128, 320), 0)
+    wc = lax.broadcasted_iota(jnp.int32, (128, 320), 1)
+    pick_out = onehot((wc == 80 * (wr // 20) + 60 + wr % 20) & (wr < 80))
+    for h in range(4):
+        out_weight[128 * h : 128 * h + 128, :] = dot(pick_out, head_weights(h)).astype(BF)
     for d in (3, 1, 2):
         remote(ysend.at[0], qkv.at[(ha + d) % 4], 24, 24 + d, {"seq": mate}).wait_recv()
         forward(d, qkv.at[(ha + d) % 4])
@@ -438,7 +447,8 @@
             return carry
 
         if finish is None:
-            lax.fori_loop(0, 2, lambda i, c: step(2 * i + 1, step(2 * i, c)), 0)
+            for i in range(4):
+                step(i, 0)
         else:
             for d in (1, 2, 3, 0):
                 step((ha + d) % 4, 0)
@@ -479,10 +489,7 @@
     def output(rows_of):
         rows = pl.ds(pl.multiple_of(rows_of * FR, FR), FR)
         mixed = jnp.concatenate([mbuf[h, rows, :] for h in range(4)], axis=1)
-        wide = dot(mixed, widen[...]).astype(BF)
-        return jnp.concatenate(
-            [dot(wide, wbuf[p].reshape(1280, wbuf.shape[3])) for p in range(2)], axis=1
-        )
+        return dot(mixed, out_weight[...])
 
     psend[...] = output(1 - core).astype(BF)
     last_swap = remote(psend, precv, 22, 22, {"seq": mate})
@@ -510,7 +517,8 @@
         out_specs=vmem,
         scratch_shapes=[
             pltpu.VMEM((rows, block), BF),
-            pltpu.VMEM((rows, block), BF),
+            pltpu.VMEM((SWAP, block), BF),
+            pltpu.VMEM((SWAP, block), BF),
             pltpu.VMEM((FR + TAIL, block + 128), BF),
             pltpu.VMEM((33, FR, 2 * CH), BF),
             pltpu.VMEM((17, FR, 2 * CH), BF),
@@ -527,6 +535,9 @@
             pltpu.VMEM(middle.shape, BF),
             pltpu.VMEM(last.shape, BF),
             pltpu.VMEM(proj.shape, BF),
+            pltpu.VMEM((16, 256, CH), BF),
+            pltpu.VMEM((4 * FR + TAIL, CH), F32),
+            pltpu.VMEM((4 * FR + TAIL, CH), F32),
             pltpu.VMEM((20, width), BF),
             pltpu.VMEM((4, 32, width), BF),
             pltpu.VMEM((2, 80, width // 2), BF),

time: 78.1 us -> 70.6 us (0.904)
  Pallas kernels: 75.5 us -> 68.1 us
    pallas_call x1, Pallas kernels: 75.5 us -> 68.1 us  [call(): pl.pallas_call(kernel, out_shape=jax.ShapeDtypeStruct((FR, width), BF), i...]
where the time goes in v4:
time: 70.6 us; the launch traced here: 70.4 us
  Pallas kernels  68.1 us (96%)
  local copies, waits for them, and re-layouts  1.72 us (2%)
    pallas_call x1, Pallas kernels, call(): pl.pallas_call(kernel, out_shape=jax.ShapeDtypeStruct((FR, width), BF), i...  68.1 us
    unnamed x1, local copies, waits for them, and re-layouts  1.72 us

profile of v4, /device:TPU:1, one launch (start us, length us, event | category | flops | bytes accessed | tf_op | source)
XLA Modules:
  0.0 70.4 jit_solution(11766286259498390571)
XLA Ops:
  0.7 68.1 %encoder.1 = bf16[128,1280]{1,0:T(8,128)(2,1)} custom-call(s32[1,1]{1,0:T(1,128)S(6)} %copy.12.length, bf16[193,2560]{1,0:T(8,128)(2,1)} %bitcast.4, bf16[20,1280]{1,0:T(8,128)(2,1)} %bitcast.5, bf16[80,512]{1,0:T(8,128)(2,1)} %first.1, bf16[4,1536,512]{2,1,0:T(8,128)(2,1)} %middle_hbm.1, bf16[2,1024,512]{2,1,0:T(8,128)(2,1)} %last_hbm.1, f32[512]{0:T(512)} %gain.1, ...), custom_call_target="tpu_custom_call" | custom-call | flops 20000000000 | bytes 20000000 | tf_op jit(solution)/shard_map/encoder/pallas_call | solution.py:511
  68.7 1.7 %copy.13 = bf16[1,128,1280]{2,1,0:T(8,128)(2,1)} copy(bf16[1,128,1280]{2,1,0:T(8,128)(2,1)} %bitcast.3) | data formatting | bytes 655360

commit v5 on v4

--- a/solution.py
+++ b/solution.py
@@ -433,17 +433,17 @@
 
     def attend(keys, values, is_first, finish=None):
         def step(i, carry):
-            s = dot(qs[i], keys)
-            top = jnp.max(s, axis=-1, keepdims=True)
-            if not is_first:
-                top = jnp.maximum(top, peak[i])
-            p = jnp.exp2(s - top)
-            o = lax.dot_general(p.astype(BF), masses(values), NT, preferred_element_type=F32)
-            if not is_first:
-                fade = jnp.exp2(peak[i] - top)
-                o = o + accum[i] * fade
-            peak[i] = top
-            accum[i] = o
+            for rows in (slice(0, 128), slice(128, 256)):
+                s = dot(qs[i, rows], keys)
+                top = jnp.max(s, axis=-1, keepdims=True)
+                if not is_first:
+                    top = jnp.maximum(top, peak[i, rows])
+                p = jnp.exp2(s - top).astype(BF)
+                o = lax.dot_general(p, masses(values), NT, preferred_element_type=F32)
+                if not is_first:
+                    o = o + accum[i, rows] * jnp.exp2(peak[i, rows] - top)
+                peak[i, rows] = top
+                accum[i, rows] = o
             return carry
 
         if finish is None:

time: 70.6 us -> 69.9 us (0.990)
  no operation moved by 1% of the time
where the time goes in v5:
time: 69.9 us; the launch traced here: 69.7 us
  Pallas kernels  67.4 us (96%)
  local copies, waits for them, and re-layouts  1.72 us (2%)
    pallas_call x1, Pallas kernels, call(): pl.pallas_call(kernel, out_shape=jax.ShapeDtypeStruct((FR, width), BF), i...  67.4 us
    unnamed x1, local copies, waits for them, and re-layouts  1.72 us

profile of v5, /device:TPU:1, one launch (start us, length us, event | category | flops | bytes accessed | tf_op | source)
XLA Modules:
  0.0 69.7 jit_solution(8674776780501798273)
XLA Ops:
  0.7 67.4 %encoder.1 = bf16[128,1280]{1,0:T(8,128)(2,1)} custom-call(s32[1,1]{1,0:T(1,128)S(6)} %copy.12.length, bf16[193,2560]{1,0:T(8,128)(2,1)} %bitcast.4, bf16[20,1280]{1,0:T(8,128)(2,1)} %bitcast.5, bf16[80,512]{1,0:T(8,128)(2,1)} %first.1, bf16[4,1536,512]{2,1,0:T(8,128)(2,1)} %middle_hbm.1, bf16[2,1024,512]{2,1,0:T(8,128)(2,1)} %last_hbm.1, f32[512]{0:T(512)} %gain.1, ...), custom_call_target="tpu_custom_call" | custom-call | flops 20000000000 | bytes 20000000 | tf_op jit(solution)/shard_map/encoder/pallas_call | solution.py:511
  68.0 1.7 %copy.13 = bf16[1,128,1280]{2,1,0:T(8,128)(2,1)} copy(bf16[1,128,1280]{2,1,0:T(8,128)(2,1)} %bitcast.3) | data formatting | bytes 655360

commit v6 on v5

--- a/solution.py
+++ b/solution.py
@@ -404,7 +404,7 @@
             forwards.append(copy)
 
     heads = []
-    for d in (0, 1, 3, 2):
+    for d in (0, 2, 1, 3):
         to = (ha + d) % 4
         project(to, 0)
         if d == 0:

time: 69.9 us -> 71.2 us (1.019)
  Pallas kernels: 67.4 us -> 68.7 us
    pallas_call x1, Pallas kernels: 67.4 us -> 68.7 us  [call(): pl.pallas_call(kernel, out_shape=jax.ShapeDtypeStruct((FR, width), BF), i...]
where the time goes in v6:
time: 71.2 us; the launch traced here: 71.1 us
  Pallas kernels  68.7 us (96%)
  local copies, waits for them, and re-layouts  1.72 us (2%)
    pallas_call x1, Pallas kernels, call(): pl.pallas_call(kernel, out_shape=jax.ShapeDtypeStruct((FR, width), BF), i...  68.7 us
    unnamed x1, local copies, waits for them, and re-layouts  1.72 us

profile of v6, /device:TPU:1, one launch (start us, length us, event | category | flops | bytes accessed | tf_op | source)
XLA Modules:
  0.0 71.1 jit_solution(9912591973271318630)
XLA Ops:
  0.7 68.7 %encoder.1 = bf16[128,1280]{1,0:T(8,128)(2,1)} custom-call(s32[1,1]{1,0:T(1,128)S(6)} %copy.12.length, bf16[193,2560]{1,0:T(8,128)(2,1)} %bitcast.4, bf16[20,1280]{1,0:T(8,128)(2,1)} %bitcast.5, bf16[80,512]{1,0:T(8,128)(2,1)} %first.1, bf16[4,1536,512]{2,1,0:T(8,128)(2,1)} %middle_hbm.1, bf16[2,1024,512]{2,1,0:T(8,128)(2,1)} %last_hbm.1, f32[512]{0:T(512)} %gain.1, ...), custom_call_target="tpu_custom_call" | custom-call | flops 20000000000 | bytes 20000000 | tf_op jit(solution)/shard_map/encoder/pallas_call | solution.py:511
  69.3 1.7 %copy.13 = bf16[1,128,1280]{2,1,0:T(8,128)(2,1)} copy(bf16[1,128,1280]{2,1,0:T(8,128)(2,1)} %bitcast.3) | data formatting | bytes 655360
